TPU v7x, 32 devices: a whole 2x2x4 slice. The times are simulated.
32 devices in a mesh: row: 8 (over z, x), col: 4 (over y, core).
Axes of the slice: x: 2, y: 2, z: 4, core: 2. Of those that a mesh axis runs over, the one named last changes fastest.
Arguments:
- weight: float32 [4096, 4096], P('row', 'col'), may hold values from -6 to 6
- blocks: float32 [5, 4096, 512], P(None, ('row', 'col')), may hold values from -0.2 to 1.2
Outputs:
- merged: float32 [4096, 4096], P('row', 'col')
All inputs are finite; a program needn't handle non-finite values.
Results may differ from a plain program's by a relative error of at most 0.00017.
Values sent between devices are 32-bit elements; how exact they have to be, the bound alone decides.
No kernel may reach another device: no remote copies, remote signals or barrier semaphores. Data moves between devices by JAX's collectives and lax.ppermute only.
A program may use at most 64 MiB of HBM per device.

v0:
```python
import jax
import jax.numpy as jnp
from jax import lax
from jax.sharding import PartitionSpec as P

FACTORS = 5


def from_partner(block, axis, stride):
    count = lax.axis_size(axis)
    route = []
    for low in range(count):
        high = low | 1 << stride
        if high != low and high < count:
            route += [(low, high), (high, low)]
    return lax.ppermute(block, axis, route)


def body(weight, blocks):
    bit_count = lax.axis_size("row").bit_length() - 1
    width = weight.shape[1]
    half_rows = weight.shape[0] // 2
    for factor in range(FACTORS):
        coefficients = lax.all_gather(blocks[factor], "col", axis=0, tiled=True)
        coefficients = coefficients.reshape(2, half_rows, 2 * half_rows)
        partner = from_partner(weight, "row", factor % bit_count)
        resident = weight.reshape(2, half_rows, width)
        partner = partner.reshape(2, half_rows, width)
        updated = jnp.einsum(
            "thj,tjc->thc",
            coefficients[:, :, :half_rows],
            resident,
            precision=lax.Precision.HIGHEST,
        )
        updated = updated + jnp.einsum(
            "thj,tjc->thc", coefficients[:, :, half_rows:], partner, precision=lax.Precision.HIGHEST
        )
        weight = updated.reshape(2 * half_rows, width)
    return weight


def solution(mesh):
    return jax.shard_map(
        body,
        mesh=mesh,
        in_specs=(P("row", "col"), P(None, ("row", "col"), None)),
        out_specs=P("row", "col"),
        check_vma=False,
    )
```

profile of v0, /device:TPU:0, one launch (start us, length us, event | category | flops | bytes accessed | tf_op | source)
XLA Modules:
  0.0 313.8 jit_solution(1661035863772956540)
XLA Ops:
  6.5 2.9 collective-permute-start
  9.5 2.3 fusion.15
  11.9 17.2 %all-gather.11.cloned.1.call-done = f32[1,512,512]{2,1,0:T(8,128)} async-done(((f32[1,128,512]{2,1,0:T(8,128)}), f32[1,512,512]{2,1,0:T(8,128)}) %all-gather.11.cloned.1.call-update) | async-done | bytes 1048592 | tf_op jit(solution)/shard_map/all_gather | solution.py:24
  29.1 3.0 fusion.13
  32.1 23.4 %collective-permute-done = f32[512,1024]{1,0:T(8,128)} collective-permute-done((f32[512,1024]{1,0:T(8,128)}, f32[512,1024]{1,0:T(8,128)}, u32[]{:S(2)}, u32[]{:S(2)}) %collective-permute-start) | collective-permute-done | bytes 2097184 | tf_op jit(solution)/shard_map/ppermute | solution.py:16
  55.5 3.5 %convolution_add_fusion.4 = f32[2,256,1024]{2,1,0:T(8,128)S(1)} fusion(f32[2,256,1024]{2,1,0:T(8,128)S(1)} %fusion.13, f32[2,256,1024]{2,1,0:T(8,128)} %bitcast.2, f32[2,256,512]{2,1,0:T(8,128)S(1)} %bitcast.46), kind=kOutput, calls=%fused_computation.4 | convolution fusion | flops 1611137024 | bytes 6815744 | tf_op jit(solution)/shard_map/thj,tjc->thc/dot_general | solution.py:35
  59.0 1.8 collective-permute-start.1
  60.9 17.1 %all-gather.13.cloned.1.call-done = f32[1,512,512]{2,1,0:T(8,128)} async-done(((f32[1,128,512]{2,1,0:T(8,128)}), f32[1,512,512]{2,1,0:T(8,128)}) %all-gather.13.cloned.1.call-update) | async-done | bytes 1048592 | tf_op jit(solution)/shard_map/all_gather | solution.py:24
  78.0 3.1 %fusion.10 = f32[2,1024,256]{1,2,0:T(8,128)S(1)} fusion(f32[2,256,1024]{2,1,0:T(8,128)S(1)} %convolution_add_fusion.4, f32[2,256,512]{2,1,0:T(8,128)} %bitcast.39), kind=kOutput, calls=%fused_computation.15 | convolution fusion | flops 1610612736 | bytes 4718592 | tf_op jit(solution)/shard_map/thj,tjc->thc/dot_general | solution.py:29
  81.1 24.9 %collective-permute-done.1 = f32[512,1024]{1,0:T(8,128)} collective-permute-done((f32[512,1024]{1,0:T(8,128)S(1)}, f32[512,1024]{1,0:T(8,128)}, u32[]{:S(2)}, u32[]{:S(2)}) %collective-permute-start.1) | collective-permute-done | bytes 2097184 | tf_op jit(solution)/shard_map/ppermute | solution.py:16
  106.0 3.7 %convolution_add_fusion.3 = f32[2,1024,256]{1,2,0:T(8,128)S(1)} fusion(f32[2,1024,256]{1,2,0:T(8,128)S(1)} %fusion.10, f32[2,256,1024]{2,1,0:T(8,128)} %bitcast.5, f32[2,256,512]{2,1,0:T(8,128)S(1)} %bitcast.40), kind=kOutput, calls=%fused_computation.3 | convolution fusion | flops 1611137024 | bytes 6815744 | tf_op jit(solution)/shard_map/thj,tjc->thc/dot_general | solution.py:35
  109.7 2.5 collective-permute-start.2
  112.5 15.9 %all-gather.15.cloned.1.call-done = f32[1,512,512]{2,1,0:T(8,128)} async-done(((f32[1,128,512]{2,1,0:T(8,128)}), f32[1,512,512]{2,1,0:T(8,128)}) %all-gather.15.cloned.1.call-update) | async-done | bytes 1048592 | tf_op jit(solution)/shard_map/all_gather | solution.py:24
  128.4 3.1 fusion.7
  131.5 70.1 %collective-permute-done.2 = f32[512,1024]{1,0:T(8,128)} collective-permute-done((f32[512,1024]{1,0:T(8,128)S(1)}, f32[512,1024]{1,0:T(8,128)}, u32[]{:S(2)}, u32[]{:S(2)}) %collective-permute-start.2) | collective-permute-done | bytes 2097184 | tf_op jit(solution)/shard_map/ppermute | solution.py:16
  201.6 3.7 %convolution_add_fusion.2 = f32[2,1024,256]{1,2,0:T(8,128)S(1)} fusion(f32[2,1024,256]{1,2,0:T(8,128)S(1)} %fusion.7, f32[2,256,1024]{2,1,0:T(8,128)} %bitcast.9, f32[2,256,512]{2,1,0:T(8,128)S(1)} %bitcast.42), kind=kOutput, calls=%fused_computation.2 | convolution fusion | flops 1611137024 | bytes 6815744 | tf_op jit(solution)/shard_map/thj,tjc->thc/dot_general | solution.py:35
  206.5 17.0 %all-gather.17.cloned.1.call-done = f32[1,512,512]{2,1,0:T(8,128)} async-done(((f32[1,128,512]{2,1,0:T(8,128)}), f32[1,512,512]{2,1,0:T(8,128)}) %all-gather.17.cloned.1.call-update) | async-done | bytes 1048592 | tf_op jit(solution)/shard_map/all_gather | solution.py:24
  223.5 3.1 fusion.4
  226.7 25.7 %collective-permute-done.3 = f32[512,1024]{1,0:T(8,128)} collective-permute-done((f32[512,1024]{1,0:T(8,128)S(1)}, f32[512,1024]{1,0:T(8,128)}, u32[]{:S(2)}, u32[]{:S(2)}) %collective-permute-start.3) | collective-permute-done | bytes 2097184 | tf_op jit(solution)/shard_map/ppermute | solution.py:16
  252.4 3.7 %convolution_add_fusion.1 = f32[2,1024,256]{1,2,0:T(8,128)S(1)} fusion(f32[2,1024,256]{1,2,0:T(8,128)S(1)} %fusion.4, f32[2,256,1024]{2,1,0:T(8,128)} %bitcast.13, f32[2,256,512]{2,1,0:T(8,128)S(1)} %bitcast.44), kind=kOutput, calls=%fused_computation.1 | convolution fusion | flops 1611137024 | bytes 6815744 | tf_op jit(solution)/shard_map/thj,tjc->thc/dot_general | solution.py:35
  256.9 18.0 %all-gather.19.cloned.1.call-done = f32[1,512,512]{2,1,0:T(8,128)} async-done(((f32[1,128,512]{2,1,0:T(8,128)}), f32[1,512,512]{2,1,0:T(8,128)}) %all-gather.19.cloned.1.call-update) | async-done | bytes 1048592 | tf_op jit(solution)/shard_map/all_gather | solution.py:24
  275.0 3.1 fusion.1
  278.1 24.2 %collective-permute-done.4 = f32[512,1024]{1,0:T(8,128)} collective-permute-done((f32[512,1024]{1,0:T(8,128)S(1)}, f32[512,1024]{1,0:T(8,128)}, u32[]{:S(2)}, u32[]{:S(2)}) %collective-permute-start.4) | collective-permute-done | bytes 2097184 | tf_op jit(solution)/shard_map/ppermute | solution.py:16
  302.3 5.0 %convolution_add_fusion = f32[2,1024,256]{1,2,0:T(8,128)} fusion(f32[2,1024,256]{1,2,0:T(8,128)S(1)} %fusion.1, f32[2,256,1024]{2,1,0:T(8,128)} %bitcast.17, f32[2,256,512]{2,1,0:T(8,128)S(1)} %bitcast.48), kind=kOutput, calls=%fused_computation | convolution fusion | flops 1611137024 | bytes 6815744 | tf_op jit(solution)/shard_map/thj,tjc->thc/dot_general | solution.py:35
  (24 shorter events, 2.4 us)
Async XLA Ops:
  6.5 22.6 %copy-start = (f32[512,1024]{1,0:T(8,128)S(1)}, f32[512,1024]{1,0:T(8,128)}, u32[]{:S(2)}) copy-start(f32[512,1024]{1,0:T(8,128)} %param.2) | copy-start | bytes 6291460
  6.5 22.6 %all-gather.11.cloned.1.call-start = ((), (), s32[]{:S(2)}) async-start(), calls=%async_computation | async-start | bytes 1310720 | tf_op jit(solution)/shard_map/all_gather | solution.py:24
  6.5 48.9 %collective-permute-start = (f32[512,1024]{1,0:T(8,128)}, f32[512,1024]{1,0:T(8,128)}, u32[]{:S(2)}, u32[]{:S(2)}) collective-permute-start(f32[512,1024]{1,0:T(8,128)} %param.2), channel_id=1, source_target_pairs={{0,4},{4,0},{8,12},{12,8},{16,20},{20,16},{24,28},{28,24},{1,5},{5... | collective-permute-start | bytes 6291464 | tf_op jit(solution)/shard_map/ppermute | solution.py:16
  11.8 66.2 %all-gather.13.cloned.1.call-start = ((), (), s32[]{:S(2)}) async-start(), calls=%async_computation.1 | async-start | bytes 1310720 | tf_op jit(solution)/shard_map/all_gather | solution.py:24
  29.1 26.4 %copy-start.4 = (f32[1,512,512]{2,1,0:T(8,128)S(1)}, f32[1,512,512]{2,1,0:T(8,128)}, u32[]{:S(2)}) copy-start(f32[1,512,512]{2,1,0:T(8,128)} %all-gather.11.cloned.1.call-done) | copy-start | bytes 3145732
  59.0 47.0 %collective-permute-start.1 = (f32[512,1024]{1,0:T(8,128)S(1)}, f32[512,1024]{1,0:T(8,128)}, u32[]{:S(2)}, u32[]{:S(2)}) collective-permute-start(f32[512,1024]{1,0:T(8,128)S(1)} %bitcast.34), channel_id=1, source_target_pairs={{0,8},{8,0},{4,12},{12,4},{16,24},{24,16},{20,28},{28,20},{1,9},{9... | collective-permute-start | bytes 6291464 | tf_op jit(solution)/shard_map/ppermute | solution.py:16
  60.9 67.5 %all-gather.15.cloned.1.call-start = ((), (), s32[]{:S(2)}) async-start(), calls=%async_computation.2 | async-start | bytes 1310720 | tf_op jit(solution)/shard_map/all_gather | solution.py:24
  78.0 28.0 %copy-start.1 = (f32[1,512,512]{2,1,0:T(8,128)S(1)}, f32[1,512,512]{2,1,0:T(8,128)}, u32[]{:S(2)}) copy-start(f32[1,512,512]{2,1,0:T(8,128)} %all-gather.13.cloned.1.call-done) | copy-start | bytes 3145732
  109.7 91.9 %collective-permute-start.2 = (f32[512,1024]{1,0:T(8,128)S(1)}, f32[512,1024]{1,0:T(8,128)}, u32[]{:S(2)}, u32[]{:S(2)}) collective-permute-start(f32[512,1024]{1,0:T(8,128)S(1)} %bitcast.35), channel_id=1, source_target_pairs={{0,16},{16,0},{4,20},{20,4},{8,24},{24,8},{12,28},{28,12},{1,17},{... | collective-permute-start | bytes 6291464 | tf_op jit(solution)/shard_map/ppermute | solution.py:16
  112.3 111.3 %all-gather.17.cloned.1.call-start = ((), (), s32[]{:S(2)}) async-start(), calls=%async_computation.3 | async-start | bytes 1310720 | tf_op jit(solution)/shard_map/all_gather | solution.py:24
  128.4 73.3 %copy-start.2 = (f32[1,512,512]{2,1,0:T(8,128)S(1)}, f32[1,512,512]{2,1,0:T(8,128)}, u32[]{:S(2)}) copy-start(f32[1,512,512]{2,1,0:T(8,128)} %all-gather.15.cloned.1.call-done) | copy-start | bytes 3145732
  205.3 47.1 %collective-permute-start.3 = (f32[512,1024]{1,0:T(8,128)S(1)}, f32[512,1024]{1,0:T(8,128)}, u32[]{:S(2)}, u32[]{:S(2)}) collective-permute-start(f32[512,1024]{1,0:T(8,128)S(1)} %bitcast.36), channel_id=1, source_target_pairs={{0,4},{4,0},{8,12},{12,8},{16,20},{20,16},{24,28},{28,24},{1,5},{5... | collective-permute-start | bytes 6291464 | tf_op jit(solution)/shard_map/ppermute | solution.py:16
  206.5 68.5 %all-gather.19.cloned.1.call-start = ((), (), s32[]{:S(2)}) async-start(), calls=%async_computation.4 | async-start | bytes 1310720 | tf_op jit(solution)/shard_map/all_gather | solution.py:24
  223.5 28.9 %copy-start.3 = (f32[1,512,512]{2,1,0:T(8,128)S(1)}, f32[1,512,512]{2,1,0:T(8,128)}, u32[]{:S(2)}) copy-start(f32[1,512,512]{2,1,0:T(8,128)} %all-gather.17.cloned.1.call-done) | copy-start | bytes 3145732
  256.1 46.2 %collective-permute-start.4 = (f32[512,1024]{1,0:T(8,128)S(1)}, f32[512,1024]{1,0:T(8,128)}, u32[]{:S(2)}, u32[]{:S(2)}) collective-permute-start(f32[512,1024]{1,0:T(8,128)S(1)} %bitcast.37), channel_id=1, source_target_pairs={{0,8},{8,0},{4,12},{12,4},{16,24},{24,16},{20,28},{28,20},{1,9},{9... | collective-permute-start | bytes 6291464 | tf_op jit(solution)/shard_map/ppermute | solution.py:16
  275.0 27.3 %copy-start.5 = (f32[1,512,512]{2,1,0:T(8,128)S(1)}, f32[1,512,512]{2,1,0:T(8,128)}, u32[]{:S(2)}) copy-start(f32[1,512,512]{2,1,0:T(8,128)} %all-gather.19.cloned.1.call-done) | copy-start | bytes 3145732
Sparse Core Ops, SparseCore 0:
  12.0 17.0 all-gather.10
  61.0 16.9 all-gather.12
  112.4 15.9 all-gather.14
  206.6 16.9 all-gather.16
  257.1 17.8 all-gather.18
where the time goes:
time: 314 us
  waiting for transfers between devices  254 us (81%)
  matrix products  35.2 us (11%)
  between operations  13.2 us (4%)
  starting transfers between devices  9.55 us (3%)
    ppermute x5, waiting for transfers between devices, from_partner(): return lax.ppermute(block, axis, route)  168 us
    all_gather x5, waiting for transfers between devices, body(): coefficients = lax.all_gather(blocks[factor], 'col', axis=0, tiled=True)  85.2 us
    dot_general x5, matrix products, body(): jnp.einsum('thj,tjc->thc', coefficients[:, :, half_rows:], partner, preci...  19.6 us
    dot_general x5, matrix products, body(): jnp.einsum('thj,tjc->thc', coefficients[:, :, :half_rows], resident, prec...  15.6 us
    ppermute x5, starting transfers between devices, from_partner(): return lax.ppermute(block, axis, route)  9.2 us
  transfers between devices with their start and end apart: 10, of which 10 were waited for; matrix products, arithmetic and copies ran while one was open for 6% of the time, Pallas kernels for 0%

commit v1 on v0

v1 whole, which is shorter than its diff:
```python
import functools

import jax
import jax.numpy as jnp
from jax import lax
from jax.experimental import pallas as pl
from jax.experimental.pallas import tpu as pltpu
from jax.sharding import PartitionSpec as P

GROUPS = 2
SPLIT = 4
STAGES = 6
FACTORS_RELAYED = (1, 2)


def partner_route(count, mask):
    return [(low, low ^ mask) for low in range(count) if low ^ mask < count]


def halves_of(values):
    high = values.astype(jnp.bfloat16)
    return high, (values - high.astype(jnp.float32)).astype(jnp.bfloat16)


def product(table, first, second):
    high = jnp.concatenate([first[0], second[0]], axis=0)
    low = jnp.concatenate([first[1], second[1]], axis=0)
    dot = functools.partial(jnp.dot, preferred_element_type=jnp.float32)
    return dot(table[0], high) + (dot(table[0], low) + dot(table[1], high))


def prepare(place, mine, mates):
    count, rows, order = mine.shape

    def kernel(place_ref, mine_ref, mates_ref, *table_refs):
        is_low = place_ref[2] == 0
        for k, table_ref in enumerate(table_refs):
            for side in range(2):
                wanted = mine_ref[k] if side == 0 else mates_ref[k]
                other = mates_ref[k] if side == 0 else mine_ref[k]
                high, low = halves_of(jnp.where(is_low, wanted, other))
                table_ref[0, side * rows : (side + 1) * rows] = high
                table_ref[1, side * rows : (side + 1) * rows] = low

    vmem = pl.BlockSpec(memory_space=pltpu.VMEM)
    return pl.pallas_call(
        kernel,
        out_shape=[jax.ShapeDtypeStruct((2, 2 * rows, order), jnp.bfloat16)] * count,
        in_specs=[pl.BlockSpec(memory_space=pltpu.SMEM), vmem, vmem],
        out_specs=[vmem] * count,
        compiler_params=pltpu.CompilerParams(vmem_limit_bytes=32 * 2**20),
        cost_estimate=pl.CostEstimate(
            flops=0, bytes_accessed=16 * count * rows * order, transcendentals=0
        ),
    )(place, mine, mates)


def step(place, weight, merged, held, arrived, tables, live, shape):
    half, width = shape
    enters, m1, m2, m3, pick, m4, m5 = live
    names, operands = [], []

    def take(name, array):
        names.append(name)
        operands.append(array)

    if m1:
        take("x0", held["x0"])
        take("x0_in", arrived["x0"])
        take("t0", tables[m1[0], 0])
    if m2:
        take("a", held["a"])
        take("o0_in", arrived["o0"])
        take("t1", tables[m2[0], 1])
        take("t1x", tables[m2[0], 1, "far"])
    if m3:
        take("m", held["m"])
        take("m_in", arrived["m"])
        take("t2", tables[m3[0], 2])
        take("t2x", tables[m3[0], 2, "far"])
    if pick:
        take("w", held["w"])
        if not m2:
            take("o0_in", arrived["o0"])
    if m4:
        take("x1", held["x1"])
        take("x1_in", arrived["x1"])
        take("t3", tables[m4[0], 3])
    if m5:
        take("o1", held["o1"])
        take("o1_in", arrived["o1"])
        take("t4", tables[m5[0], 4])

    out_names = []
    if enters:
        out_names.append("x0")
    if m1:
        out_names.append("a")
    if m1 or m3:
        out_names.append("o0")
    if m2:
        out_names.append("m")
    if m3:
        out_names.append("w")
    if pick:
        out_names.append("x1")
    if m4:
        out_names.append("o1")
    sizes = {name: ((2,) if name == "m" else ()) + (half, width) for name in out_names}

    def kernel(place_ref, weight_ref, merged_ref, *refs):
        ins = dict(zip(names, refs))
        refs = refs[len(names) :]
        merged_out, outs = refs[0], dict(zip(out_names, refs[1:]))
        refs = refs[1 + len(out_names) :]
        inner = place_ref[3] == 1

        def region(ref, chunk):
            rows = pl.ds(pl.multiple_of(place_ref[chunk[0]] * half, half), half)
            return ref.at[rows, pl.ds(chunk[1] * width, width)]

        if enters:
            entering = pltpu.make_async_copy(region(weight_ref, enters), outs["x0"], refs[-1].at[0])
            entering.start()
        if m5:
            result = refs[0]
            result[...] = product(
                ins["t4"], halves_of(ins["o1"][...]), halves_of(ins["o1_in"][...])
            )
            leaving = pltpu.make_async_copy(result, region(merged_out, m5), refs[-1].at[1])
            leaving.start()
        if m2 or m3:

            @pl.when(inner)
            def _():
                if m3:
                    mine, far = halves_of(ins["m"][0]), halves_of(ins["m"][1])
                    theirs, theirs_far = halves_of(ins["m_in"][0]), halves_of(ins["m_in"][1])
                    outs["o0"][...] = product(ins["t2x"], far, theirs)
                    outs["w"][...] = product(ins["t2"], mine, theirs_far)
                if m2:
                    mine, far = halves_of(ins["a"][...]), halves_of(ins["o0_in"][...])
                    outs["m"][0] = product(ins["t1"], mine, far)
                    outs["m"][1] = product(ins["t1x"], far, mine)

        if pick:
            outs["x1"][...] = jnp.where(inner, ins["w"][...], ins["o0_in"][...])
        if m4:
            outs["o1"][...] = product(
                ins["t3"], halves_of(ins["x1"][...]), halves_of(ins["x1_in"][...])
            )
        if m1:
            mixed = product(ins["t0"], halves_of(ins["x0"][...]), halves_of(ins["x0_in"][...]))
            outs["a"][...] = mixed

            @pl.when(jnp.logical_not(inner))
            def _():
                outs["o0"][...] = mixed

        if enters:
            entering.wait()
        if m5:
            leaving.wait()

    any_space = pl.BlockSpec(memory_space=pl.ANY)
    vmem = pl.BlockSpec(memory_space=pltpu.VMEM)
    scratch = [pltpu.VMEM((half, width), jnp.float32)] if m5 else []
    products = sum(map(bool, (m1, m2, m2, m3, m3, m4, m5)))
    first_merged = merged is None
    head = [weight] if first_merged else [weight, merged]
    body_of = kernel
    if first_merged:
        body_of = lambda place_ref, weight_ref, *refs: kernel(place_ref, weight_ref, None, *refs)
    merged, *results = pl.pallas_call(
        body_of,
        out_shape=[jax.ShapeDtypeStruct(weight.shape, jnp.float32)]
        + [jax.ShapeDtypeStruct(sizes[name], jnp.float32) for name in out_names],
        in_specs=[pl.BlockSpec(memory_space=pltpu.SMEM)]
        + [any_space] * len(head)
        + [vmem] * len(operands),
        out_specs=[any_space] + [vmem] * len(out_names),
        scratch_shapes=scratch + [pltpu.SemaphoreType.DMA((2,))],
        input_output_aliases={} if first_merged else {2: 0},
        compiler_params=pltpu.CompilerParams(vmem_limit_bytes=32 * 2**20),
        cost_estimate=pl.CostEstimate(
            flops=products * 12 * half * half * width,
            bytes_accessed=4 * half * width * (2 + len(names) + len(out_names)),
            transcendentals=0,
        ),
    )(place, *head, *operands)
    return merged, dict(zip(out_names, results))


def relayed(weight, blocks):
    count = lax.axis_size("row")
    columns = lax.axis_size("col")
    half = blocks.shape[2] // 2
    width = weight.shape[1] // SPLIT
    row, col = lax.axis_index("row"), lax.axis_index("col")
    own = col // 2
    is_inner = lambda r: (r >> 1 & 1) != (r >> 2 & 1)
    inner = jnp.where(is_inner(row), 1, 0)
    place = jnp.stack([own, 1 - own, col % 2, inner]).astype(jnp.int32)

    along_x = partner_route(count, 1)
    out_in = [(r, r ^ 2) for r in range(count) if not is_inner(r)]
    in_out = [(r, r ^ 2) for r in range(count) if is_inner(r)]
    middle = [(r, r ^ 6) for r in range(count) if is_inner(r)]
    cores = partner_route(columns, 1)
    across = partner_route(columns, 2)

    far = lax.ppermute(jnp.stack([blocks[k] for k in FACTORS_RELAYED]), "row", out_in)
    mates = lax.ppermute(blocks, "col", cores)
    across_blocks = lax.ppermute(blocks, "col", across)
    far_mates = lax.ppermute(far, "col", cores)
    across_far = lax.ppermute(far, "col", across)
    across_mates = lax.ppermute(across_blocks, "col", cores)
    across_far_mates = lax.ppermute(across_far, "col", cores)
    tables = {}
    for t, near_pair, far_pair in (
        (0, (blocks, mates), (far, far_mates)),
        (1, (across_blocks, across_mates), (across_far, across_far_mates)),
    ):
        for k, table in enumerate(prepare(place, *near_pair)):
            tables[t, k] = table
        for k, table in zip(FACTORS_RELAYED, prepare(place, *far_pair)):
            tables[t, k, "far"] = table

    per_group = SPLIT // GROUPS
    queues = [
        [(t, group * per_group + piece) for t in range(2) for piece in range(per_group)]
        for group in range(GROUPS)
    ]
    length = len(queues[0])
    merged = None
    held = [{} for _ in queues]
    arrived = [{} for _ in queues]
    for tick in range(length + STAGES):
        for group, queue in enumerate(queues):
            live = [
                queue[tick - stage] if 0 <= tick - stage < length else None
                for stage in range(STAGES + 1)
            ]
            merged, now = step(
                place, weight, merged, held[group], arrived[group], tables, live, (half, width)
            )
            held[group] = now
            enters, m1, m2, m3, pick, m4, m5 = live
            new = {}
            if m2:
                new["m"] = lax.ppermute(now["m"], "row", middle)
            if "o0" in now:
                route = (out_in if m1 else []) + (in_out if m3 else [])
                new["o0"] = lax.ppermute(now["o0"], "row", route)
            if "o1" in now:
                new["o1"] = lax.ppermute(now["o1"], "row", out_in + in_out)
            for name in ("x0", "x1"):
                if name in now:
                    new[name] = lax.ppermute(now[name], "row", along_x)
            arrived[group] = new
    return merged


def plain(weight, blocks):
    count = lax.axis_size("row")
    bit_count = count.bit_length() - 1
    factors = blocks.shape[0]
    half = blocks.shape[2] // 2
    halves = weight.shape[0] // half
    tables = [lax.all_gather(blocks[k], "col", axis=0, tiled=True) for k in range(factors)]
    bands = []
    for t in range(halves):
        rows = slice(t * half, (t + 1) * half)
        held = weight[rows]
        for factor in range(factors):
            table = tables[factor][rows]
            partner = lax.ppermute(held, "row", partner_route(count, 1 << factor % bit_count))
            dot = functools.partial(jnp.dot, precision=lax.Precision.HIGHEST)
            held = dot(table[:, :half], held) + dot(table[:, half:], partner)
        bands.append(held)
    return jnp.concatenate(bands, axis=0)


def body(weight, blocks):
    fits = lax.axis_size("row") == 8 and lax.axis_size("col") == 4
    fits = fits and weight.shape[0] == blocks.shape[2] == 4 * blocks.shape[1]
    return (relayed if fits else plain)(weight, blocks)


def solution(mesh):
    return jax.shard_map(
        body,
        mesh=mesh,
        in_specs=(P("row", "col"), P(None, ("row", "col"), None)),
        out_specs=P("row", "col"),
        check_vma=False,
    )
```

time: 314 us -> 197 us (0.63)
  waiting for transfers between devices: 254 us -> 63.8 us
  starting transfers between devices: 9.55 us -> 98.2 us
  matrix products: 35.2 us -> 0 us
  Pallas kernels: 0 us -> 30.3 us
  between operations: 13.2 us -> 0.63 us
    ppermute x5 -> x51, waiting for transfers between devices: 168 us -> 63.8 us  [the longest x1 24.4 us: relayed(): across_blocks = lax.ppermute(blocks, 'col', across)]
    ppermute x5 -> x51, starting transfers between devices: 9.2 us -> 98.2 us  [the longest x12 46.9 us: relayed(): new['o0'] = lax.ppermute(now['o0'], 'row', route)]
    all_gather x5 -> x0, waiting for transfers between devices: 85.2 us -> none  [body(): coefficients = lax.all_gather(blocks[factor], 'col', axis=0, tiled=True)]
    dot_general x10 -> x0, matrix products: 35.2 us -> none  [the longest x5 19.6 us: body(): jnp.einsum('thj,tjc->thc', coefficients[:, :, half_rows:], partner, preci...]
    pallas_call x0 -> x24, Pallas kernels: none -> 30.3 us  [the longest x20 25.1 us: step(): pl.pallas_call(body_of, out_shape=[jax.ShapeDtypeStruct(weight.shape, jnp...]
  transfers between devices with their start and end apart: 10 -> 51, of which waited for: 10 -> 19; matrix products, arithmetic and copies ran while one was open for 6% -> 1% of each run, Pallas kernels for 0% -> 15%
where the time goes in v1:
time: 197 us; the launch traced here: 196 us
  starting transfers between devices  98.2 us (50%)
  waiting for transfers between devices  63.8 us (32%)
  Pallas kernels  30.3 us (15%)
  local copies, waits for them, and re-layouts  3.04 us (2%)
    ppermute x12, starting transfers between devices, relayed(): new['o0'] = lax.ppermute(now['o0'], 'row', route)  46.9 us
    pallas_call x20, Pallas kernels, step(): pl.pallas_call(body_of, out_shape=[jax.ShapeDtypeStruct(weight.shape, jnp...  25.1 us
    ppermute x1, waiting for transfers between devices, relayed(): across_blocks = lax.ppermute(blocks, 'col', across)  24.4 us
    ppermute x8, waiting for transfers between devices, relayed(): new['o1'] = lax.ppermute(now['o1'], 'row', out_in + in_out)  23.3 us
    ppermute x16, starting transfers between devices, relayed(): new[name] = lax.ppermute(now[name], 'row', along_x)  21.1 us
    ppermute x8, starting transfers between devices, relayed(): new['o1'] = lax.ppermute(now['o1'], 'row', out_in + in_out)  15.8 us
    ppermute x12, waiting for transfers between devices, relayed(): new['o0'] = lax.ppermute(now['o0'], 'row', route)  8.28 us
    ppermute x16, waiting for transfers between devices, relayed(): new[name] = lax.ppermute(now[name], 'row', along_x)  7.79 us
  transfers between devices with their start and end apart: 51, of which 19 were waited for; matrix products, arithmetic and copies ran while one was open for 1% of the time, Pallas kernels for 15%

profile of v1, /device:TPU:0, one launch (start us, length us, event | category | flops | bytes accessed | tf_op | source)
XLA Modules:
  0.0 196.0 jit_solution(3191397101544373445)
XLA Ops:
  0.0 3.0 %collective-permute-start.10 = (f32[5,128,512]{2,1,0:T(8,128)}, f32[5,128,512]{2,1,0:T(8,128)S(1)}, u32[]{:S(2)}, u32[]{:S(2)}) collective-permute-start(f32[5,128,512]{2,1,0:T(8,128)} %mine_ref.1), channel_id=1, source_target_pairs={{0,2},{1,3},{2,0},{3,1},{4,6},{5,7},{6,4},{7,5},{8,10},{9,11},{10,... | collective-permute-start | bytes 3932168 | tf_op jit(solution)/shard_map/ppermute | solution.py:214
  4.1 3.5 %collective-permute-start.5 = (f32[2,128,512]{2,1,0:T(8,128)S(1)}, f32[2,128,512]{2,1,0:T(8,128)S(1)}, u32[]{:S(2)}, u32[]{:S(2)}) collective-permute-start(f32[2,128,512]{2,1,0:T(8,128)S(1)} %stack.23), channel_id=1, source_target_pairs={{0,8},{4,12},{24,16},{28,20},{1,9},{5,13},{25,17},{29,21},{2,10},{... | collective-permute-start | bytes 1572872 | tf_op jit(solution)/shard_map/ppermute | solution.py:212
  7.6 24.4 %collective-permute-done.10.mine_ref = f32[5,128,512]{2,1,0:T(8,128)S(1)} collective-permute-done((f32[5,128,512]{2,1,0:T(8,128)}, f32[5,128,512]{2,1,0:T(8,128)S(1)}, u32[]{:S(2)}, u32[]{:S(2)}) %collective-permute-start.10) | collective-permute-done | bytes 1310752 | tf_op jit(solution)/shard_map/ppermute | solution.py:214
  37.8 1.9 shard_map.30
  39.8 4.2 %collective-permute-done.refs_1_ = f32[256,256]{1,0:T(8,128)S(1)} collective-permute-done((f32[256,256]{1,0:T(8,128)S(1)}, f32[256,256]{1,0:T(8,128)S(1)}, u32[]{:S(2)}, u32[]{:S(2)}) %collective-permute-start) | collective-permute-done | bytes 262176 | tf_op jit(solution)/shard_map/ppermute | solution.py:259
  46.7 3.5 %collective-permute-start.4 = (f32[256,256]{1,0:T(8,128)S(1)}, f32[256,256]{1,0:T(8,128)S(1)}, u32[]{:S(2)}, u32[]{:S(2)}) collective-permute-start(f32[256,256]{1,0:T(8,128)S(1)} %get-tuple-element.106), channel_id=1, source_target_pairs={{0,8},{4,12},{24,16},{28,20},{1,9},{5,13},{25,17},{29,21},{2,10},{... | collective-permute-start | bytes 786440 | tf_op jit(solution)/shard_map/ppermute | solution.py:254
  54.7 4.2 %collective-permute-start.8 = (f32[256,256]{1,0:T(8,128)S(1)}, f32[256,256]{1,0:T(8,128)S(1)}, u32[]{:S(2)}, u32[]{:S(2)}) collective-permute-start(f32[256,256]{1,0:T(8,128)S(1)} %get-tuple-element.112), channel_id=1, source_target_pairs={{0,8},{4,12},{24,16},{28,20},{1,9},{5,13},{25,17},{29,21},{2,10},{... | collective-permute-start | bytes 786440 | tf_op jit(solution)/shard_map/ppermute | solution.py:254
  60.6 4.7 %collective-permute-start.12 = (f32[256,256]{1,0:T(8,128)S(1)}, f32[256,256]{1,0:T(8,128)S(1)}, u32[]{:S(2)}, u32[]{:S(2)}) collective-permute-start(f32[256,256]{1,0:T(8,128)S(1)} %get-tuple-element.117), channel_id=1, source_target_pairs={{0,8},{4,12},{24,16},{28,20},{1,9},{5,13},{25,17},{29,21},{2,10},{... | collective-permute-start | bytes 786440 | tf_op jit(solution)/shard_map/ppermute | solution.py:254
  71.8 3.9 %collective-permute-start.15 = (f32[256,256]{1,0:T(8,128)S(1)}, f32[256,256]{1,0:T(8,128)S(1)}, u32[]{:S(2)}, u32[]{:S(2)}) collective-permute-start(f32[256,256]{1,0:T(8,128)S(1)} %get-tuple-element.124), channel_id=1, source_target_pairs={{0,8},{4,12},{24,16},{28,20},{1,9},{5,13},{25,17},{29,21},{2,10},{... | collective-permute-start | bytes 786440 | tf_op jit(solution)/shard_map/ppermute | solution.py:254
  79.1 2.5 %collective-permute-done.15.refs_4_ = f32[256,256]{1,0:T(8,128)S(1)} collective-permute-done((f32[256,256]{1,0:T(8,128)S(1)}, f32[256,256]{1,0:T(8,128)S(1)}, u32[]{:S(2)}, u32[]{:S(2)}) %collective-permute-start.15) | collective-permute-done | bytes 262176 | tf_op jit(solution)/shard_map/ppermute | solution.py:254
  81.6 2.5 %collective-permute-start.18 = (f32[256,256]{1,0:T(8,128)S(1)}, f32[256,256]{1,0:T(8,128)S(1)}, u32[]{:S(2)}, u32[]{:S(2)}) collective-permute-start(f32[256,256]{1,0:T(8,128)S(1)} %get-tuple-element.129), channel_id=1, source_target_pairs={{0,8},{4,12},{24,16},{28,20},{8,0},{12,4},{16,24},{20,28},{1,9},{5... | collective-permute-start | bytes 786440 | tf_op jit(solution)/shard_map/ppermute | solution.py:254
  88.0 7.7 %collective-permute-start.23 = (f32[256,256]{1,0:T(8,128)S(1)}, f32[256,256]{1,0:T(8,128)S(1)}, u32[]{:S(2)}, u32[]{:S(2)}) collective-permute-start(f32[256,256]{1,0:T(8,128)S(1)} %get-tuple-element.137), channel_id=1, source_target_pairs={{0,8},{4,12},{24,16},{28,20},{8,0},{12,4},{16,24},{20,28},{1,9},{5... | collective-permute-start | bytes 786440 | tf_op jit(solution)/shard_map/ppermute | solution.py:254
  97.5 7.3 %collective-permute-start.25 = (f32[256,256]{1,0:T(8,128)S(1)}, f32[256,256]{1,0:T(8,128)S(1)}, u32[]{:S(2)}, u32[]{:S(2)}) collective-permute-start(f32[256,256]{1,0:T(8,128)S(1)} %get-tuple-element.142), channel_id=1, source_target_pairs={{0,8},{4,12},{24,16},{28,20},{8,0},{12,4},{16,24},{20,28},{1,9},{5... | collective-permute-start | bytes 786440 | tf_op jit(solution)/shard_map/ppermute | solution.py:254
  107.9 8.0 %collective-permute-start.28 = (f32[256,256]{1,0:T(8,128)S(1)}, f32[256,256]{1,0:T(8,128)S(1)}, u32[]{:S(2)}, u32[]{:S(2)}) collective-permute-start(f32[256,256]{1,0:T(8,128)S(1)} %get-tuple-element.151), channel_id=1, source_target_pairs={{0,8},{4,12},{24,16},{28,20},{8,0},{12,4},{16,24},{20,28},{1,9},{5... | collective-permute-start | bytes 786440 | tf_op jit(solution)/shard_map/ppermute | solution.py:254
  122.5 7.7 %collective-permute-start.34 = (f32[256,256]{1,0:T(8,128)S(1)}, f32[256,256]{1,0:T(8,128)S(1)}, u32[]{:S(2)}, u32[]{:S(2)}) collective-permute-start(f32[256,256]{1,0:T(8,128)S(1)} %get-tuple-element.160.refs_9_), channel_id=1, source_target_pairs={{0,8},{4,12},{24,16},{28,20},{8,0},{12,4},{16,24},{20,28},{1,9},{5... | collective-permute-start | bytes 786440 | tf_op jit(solution)/shard_map/ppermute | solution.py:256
  136.8 4.5 %collective-permute-start.38 = (f32[256,256]{1,0:T(8,128)S(1)}, f32[256,256]{1,0:T(8,128)S(1)}, u32[]{:S(2)}, u32[]{:S(2)}) collective-permute-start(f32[256,256]{1,0:T(8,128)S(1)} %get-tuple-element.167.refs_9_), channel_id=1, source_target_pairs={{0,8},{4,12},{24,16},{28,20},{8,0},{12,4},{16,24},{20,28},{1,9},{5... | collective-permute-start | bytes 786440 | tf_op jit(solution)/shard_map/ppermute | solution.py:256
  148.9 2.3 %collective-permute-done.38.refs_10_ = f32[256,256]{1,0:T(8,128)S(1)} collective-permute-done((f32[256,256]{1,0:T(8,128)S(1)}, f32[256,256]{1,0:T(8,128)S(1)}, u32[]{:S(2)}, u32[]{:S(2)}) %collective-permute-start.38) | collective-permute-done | bytes 262176 | tf_op jit(solution)/shard_map/ppermute | solution.py:256
  158.4 4.1 %collective-permute-done.41.refs_6_ = f32[256,256]{1,0:T(8,128)S(1)} collective-permute-done((f32[256,256]{1,0:T(8,128)S(1)}, f32[256,256]{1,0:T(8,128)S(1)}, u32[]{:S(2)}, u32[]{:S(2)}) %collective-permute-start.41) | collective-permute-done | bytes 262176 | tf_op jit(solution)/shard_map/ppermute | solution.py:256
  162.5 1.9 shard_map.46
  166.0 2.1 %collective-permute-done.42.refs_1_ = f32[256,256]{1,0:T(8,128)S(1)} collective-permute-done((f32[256,256]{1,0:T(8,128)S(1)}, f32[256,256]{1,0:T(8,128)S(1)}, u32[]{:S(2)}, u32[]{:S(2)}) %collective-permute-start.42) | collective-permute-done | bytes 262176 | tf_op jit(solution)/shard_map/ppermute | solution.py:254
  168.1 5.3 %collective-permute-done.44.refs_6_ = f32[256,256]{1,0:T(8,128)S(1)} collective-permute-done((f32[256,256]{1,0:T(8,128)S(1)}, f32[256,256]{1,0:T(8,128)S(1)}, u32[]{:S(2)}, u32[]{:S(2)}) %collective-permute-start.44) | collective-permute-done | bytes 262176 | tf_op jit(solution)/shard_map/ppermute | solution.py:256
  173.4 1.9 shard_map.47
  181.8 4.1 %collective-permute-done.48.refs_4_ = f32[256,256]{1,0:T(8,128)S(1)} collective-permute-done((f32[256,256]{1,0:T(8,128)S(1)}, f32[256,256]{1,0:T(8,128)S(1)}, u32[]{:S(2)}, u32[]{:S(2)}) %collective-permute-start.48) | collective-permute-done | bytes 262176 | tf_op jit(solution)/shard_map/ppermute | solution.py:256
  190.8 3.3 %collective-permute-done.50.refs_1_ = f32[256,256]{1,0:T(8,128)S(1)} collective-permute-done((f32[256,256]{1,0:T(8,128)S(1)}, f32[256,256]{1,0:T(8,128)S(1)}, u32[]{:S(2)}, u32[]{:S(2)}) %collective-permute-start.50) | collective-permute-done | bytes 262176 | tf_op jit(solution)/shard_map/ppermute | solution.py:256
  (110 shorter events, 76.9 us)
Async XLA Ops:
  0.0 32.0 %collective-permute-start.10 = (f32[5,128,512]{2,1,0:T(8,128)}, f32[5,128,512]{2,1,0:T(8,128)S(1)}, u32[]{:S(2)}, u32[]{:S(2)}) collective-permute-start(f32[5,128,512]{2,1,0:T(8,128)} %mine_ref.1), channel_id=1, source_target_pairs={{0,2},{1,3},{2,0},{3,1},{4,6},{5,7},{6,4},{7,5},{8,10},{9,11},{10,... | collective-permute-start | bytes 3932168 | tf_op jit(solution)/shard_map/ppermute | solution.py:214
  3.0 34.5 %collective-permute-start.1 = (f32[5,128,512]{2,1,0:T(8,128)}, f32[5,128,512]{2,1,0:T(8,128)}, u32[]{:S(2)}, u32[]{:S(2)}) collective-permute-start(f32[5,128,512]{2,1,0:T(8,128)} %mine_ref.1), channel_id=1, source_target_pairs={{0,1},{1,0},{2,3},{3,2},{4,5},{5,4},{6,7},{7,6},{8,9},{9,8},{10,11... | collective-permute-start | bytes 3932168 | tf_op jit(solution)/shard_map/ppermute | solution.py:213
  4.1 27.9 %collective-permute-start.5 = (f32[2,128,512]{2,1,0:T(8,128)S(1)}, f32[2,128,512]{2,1,0:T(8,128)S(1)}, u32[]{:S(2)}, u32[]{:S(2)}) collective-permute-start(f32[2,128,512]{2,1,0:T(8,128)S(1)} %stack.23), channel_id=1, source_target_pairs={{0,8},{4,12},{24,16},{28,20},{1,9},{5,13},{25,17},{29,21},{2,10},{... | collective-permute-start | bytes 1572872 | tf_op jit(solution)/shard_map/ppermute | solution.py:212
  32.0 36.6 %collective-permute-start.11 = (f32[5,128,512]{2,1,0:T(8,128)S(1)}, f32[5,128,512]{2,1,0:T(8,128)S(1)}, u32[]{:S(2)}, u32[]{:S(2)}) collective-permute-start(f32[5,128,512]{2,1,0:T(8,128)S(1)} %collective-permute-done.10.mine_ref), channel_id=1, source_target_pairs={{0,1},{1,0},{2,3},{3,2},{4,5},{5,4},{6,7},{7,6},{8,9},{9,8},{10,11... | collective-permute-start | bytes 3932168 | tf_op jit(solution)/shard_map/ppermute | solution.py:217
  32.0 18.3 %collective-permute-start.6 = (f32[2,128,512]{2,1,0:T(8,128)S(1)}, f32[2,128,512]{2,1,0:T(8,128)}, u32[]{:S(2)}, u32[]{:S(2)}) collective-permute-start(f32[2,128,512]{2,1,0:T(8,128)S(1)} %collective-permute-done.5.mine_ref), channel_id=1, source_target_pairs={{0,1},{1,0},{2,3},{3,2},{4,5},{5,4},{6,7},{7,6},{8,9},{9,8},{10,11... | collective-permute-start | bytes 1572872 | tf_op jit(solution)/shard_map/ppermute | solution.py:215
  37.1 16.0 %collective-permute-start.2 = (f32[256,256]{1,0:T(8,128)S(1)}, f32[256,256]{1,0:T(8,128)S(1)}, u32[]{:S(2)}, u32[]{:S(2)}) collective-permute-start(f32[256,256]{1,0:T(8,128)S(1)} %get-tuple-element.102.refs_0_), channel_id=1, source_target_pairs={{0,4},{4,0},{8,12},{12,8},{16,20},{20,16},{24,28},{28,24},{1,5},{5... | collective-permute-start | bytes 786440 | tf_op jit(solution)/shard_map/ppermute | solution.py:259
  50.2 17.6 %collective-permute-start.19 = (f32[2,128,512]{2,1,0:T(8,128)S(1)}, f32[2,128,512]{2,1,0:T(8,128)S(1)}, u32[]{:S(2)}, u32[]{:S(2)}) collective-permute-start(f32[2,128,512]{2,1,0:T(8,128)S(1)} %collective-permute-done.5.mine_ref), channel_id=1, source_target_pairs={{0,2},{1,3},{2,0},{3,1},{4,6},{5,7},{6,4},{7,5},{8,10},{9,11},{10,... | collective-permute-start | bytes 1572872 | tf_op jit(solution)/shard_map/ppermute | solution.py:216
  59.9 15.8 %collective-permute-start.13 = (f32[2,256,256]{2,1,0:T(8,128)S(1)}, f32[2,256,256]{2,1,0:T(8,128)S(1)}, u32[]{:S(2)}, u32[]{:S(2)}) collective-permute-start(f32[2,256,256]{2,1,0:T(8,128)S(1)} %get-tuple-element.118.refs_7_), channel_id=1, source_target_pairs={{8,16},{12,20},{16,8},{20,12},{9,17},{13,21},{17,9},{21,13},{10,18... | collective-permute-start | bytes 1572872 | tf_op jit(solution)/shard_map/ppermute | solution.py:251
  67.9 16.2 %collective-permute-start.16 = (f32[2,256,256]{2,1,0:T(8,128)S(1)}, f32[2,256,256]{2,1,0:T(8,128)S(1)}, u32[]{:S(2)}, u32[]{:S(2)}) collective-permute-start(f32[2,256,256]{2,1,0:T(8,128)S(1)} %get-tuple-element.125.refs_7_), channel_id=1, source_target_pairs={{8,16},{12,20},{16,8},{20,12},{9,17},{13,21},{17,9},{21,13},{10,18... | collective-permute-start | bytes 1572872 | tf_op jit(solution)/shard_map/ppermute | solution.py:251
  68.6 17.2 %collective-permute-start.20 = (f32[2,128,512]{2,1,0:T(8,128)S(1)}, f32[2,128,512]{2,1,0:T(8,128)S(1)}, u32[]{:S(2)}, u32[]{:S(2)}) collective-permute-start(f32[2,128,512]{2,1,0:T(8,128)S(1)} %collective-permute-done.19.mine_ref), channel_id=1, source_target_pairs={{0,1},{1,0},{2,3},{3,2},{4,5},{5,4},{6,7},{7,6},{8,9},{9,8},{10,11... | collective-permute-start | bytes 1572872 | tf_op jit(solution)/shard_map/ppermute | solution.py:218
  76.7 19.0 %collective-permute-start.21 = (f32[2,256,256]{2,1,0:T(8,128)S(1)}, f32[2,256,256]{2,1,0:T(8,128)S(1)}, u32[]{:S(2)}, u32[]{:S(2)}) collective-permute-start(f32[2,256,256]{2,1,0:T(8,128)S(1)} %get-tuple-element.132.refs_7_), channel_id=1, source_target_pairs={{8,16},{12,20},{16,8},{20,12},{9,17},{13,21},{17,9},{21,13},{10,18... | collective-permute-start | bytes 1572872 | tf_op jit(solution)/shard_map/ppermute | solution.py:251
  85.1 21.1 %collective-permute-start.24 = (f32[2,256,256]{2,1,0:T(8,128)S(1)}, f32[2,256,256]{2,1,0:T(8,128)S(1)}, u32[]{:S(2)}, u32[]{:S(2)}) collective-permute-start(f32[2,256,256]{2,1,0:T(8,128)S(1)} %get-tuple-element.138.refs_7_), channel_id=1, source_target_pairs={{8,16},{12,20},{16,8},{20,12},{9,17},{13,21},{17,9},{21,13},{10,18... | collective-permute-start | bytes 1572872 | tf_op jit(solution)/shard_map/ppermute | solution.py:251
  86.6 18.1 %collective-permute-start.22 = (f32[256,256]{1,0:T(8,128)S(1)}, f32[256,256]{1,0:T(8,128)S(1)}, u32[]{:S(2)}, u32[]{:S(2)}) collective-permute-start(f32[256,256]{1,0:T(8,128)S(1)} %get-tuple-element.135.refs_0_), channel_id=1, source_target_pairs={{0,4},{4,0},{8,12},{12,8},{16,20},{20,16},{24,28},{28,24},{1,5},{5... | collective-permute-start | bytes 786440 | tf_op jit(solution)/shard_map/ppermute | solution.py:259
  88.0 18.2 %collective-permute-start.23 = (f32[256,256]{1,0:T(8,128)S(1)}, f32[256,256]{1,0:T(8,128)S(1)}, u32[]{:S(2)}, u32[]{:S(2)}) collective-permute-start(f32[256,256]{1,0:T(8,128)S(1)} %get-tuple-element.137), channel_id=1, source_target_pairs={{0,8},{4,12},{24,16},{28,20},{8,0},{12,4},{16,24},{20,28},{1,9},{5... | collective-permute-start | bytes 786440 | tf_op jit(solution)/shard_map/ppermute | solution.py:254
  96.8 20.7 %collective-permute-start.26 = (f32[2,256,256]{2,1,0:T(8,128)S(1)}, f32[2,256,256]{2,1,0:T(8,128)S(1)}, u32[]{:S(2)}, u32[]{:S(2)}) collective-permute-start(f32[2,256,256]{2,1,0:T(8,128)S(1)} %get-tuple-element.143.refs_4_), channel_id=1, source_target_pairs={{8,16},{12,20},{16,8},{20,12},{9,17},{13,21},{17,9},{21,13},{10,18... | collective-permute-start | bytes 1572872 | tf_op jit(solution)/shard_map/ppermute | solution.py:251
  97.5 18.5 %collective-permute-start.25 = (f32[256,256]{1,0:T(8,128)S(1)}, f32[256,256]{1,0:T(8,128)S(1)}, u32[]{:S(2)}, u32[]{:S(2)}) collective-permute-start(f32[256,256]{1,0:T(8,128)S(1)} %get-tuple-element.142), channel_id=1, source_target_pairs={{0,8},{4,12},{24,16},{28,20},{8,0},{12,4},{16,24},{20,28},{1,9},{5... | collective-permute-start | bytes 786440 | tf_op jit(solution)/shard_map/ppermute | solution.py:254
  107.2 22.9 %collective-permute-start.29 = (f32[2,256,256]{2,1,0:T(8,128)S(1)}, f32[2,256,256]{2,1,0:T(8,128)S(1)}, u32[]{:S(2)}, u32[]{:S(2)}) collective-permute-start(f32[2,256,256]{2,1,0:T(8,128)S(1)} %get-tuple-element.152.refs_4_), channel_id=1, source_target_pairs={{8,16},{12,20},{16,8},{20,12},{9,17},{13,21},{17,9},{21,13},{10,18... | collective-permute-start | bytes 1572872 | tf_op jit(solution)/shard_map/ppermute | solution.py:251
  118.4 22.8 %collective-permute-start.31 = (f32[2,256,256]{2,1,0:T(8,128)S(1)}, f32[2,256,256]{2,1,0:T(8,128)S(1)}, u32[]{:S(2)}, u32[]{:S(2)}) collective-permute-start(f32[2,256,256]{2,1,0:T(8,128)S(1)} %get-tuple-element.156.refs_0_), channel_id=1, source_target_pairs={{8,16},{12,20},{16,8},{20,12},{9,17},{13,21},{17,9},{21,13},{10,18... | collective-permute-start | bytes 1572872 | tf_op jit(solution)/shard_map/ppermute | solution.py:251
  122.5 14.3 %collective-permute-start.34 = (f32[256,256]{1,0:T(8,128)S(1)}, f32[256,256]{1,0:T(8,128)S(1)}, u32[]{:S(2)}, u32[]{:S(2)}) collective-permute-start(f32[256,256]{1,0:T(8,128)S(1)} %get-tuple-element.160.refs_9_), channel_id=1, source_target_pairs={{0,8},{4,12},{24,16},{28,20},{8,0},{12,4},{16,24},{20,28},{1,9},{5... | collective-permute-start | bytes 786440 | tf_op jit(solution)/shard_map/ppermute | solution.py:256
  131.2 20.1 %collective-permute-start.35 = (f32[2,256,256]{2,1,0:T(8,128)S(1)}, f32[2,256,256]{2,1,0:T(8,128)S(1)}, u32[]{:S(2)}, u32[]{:S(2)}) collective-permute-start(f32[2,256,256]{2,1,0:T(8,128)S(1)} %get-tuple-element.163.refs_0_), channel_id=1, source_target_pairs={{8,16},{12,20},{16,8},{20,12},{9,17},{13,21},{17,9},{21,13},{10,18... | collective-permute-start | bytes 1572872 | tf_op jit(solution)/shard_map/ppermute | solution.py:251
  136.8 14.5 %collective-permute-start.38 = (f32[256,256]{1,0:T(8,128)S(1)}, f32[256,256]{1,0:T(8,128)S(1)}, u32[]{:S(2)}, u32[]{:S(2)}) collective-permute-start(f32[256,256]{1,0:T(8,128)S(1)} %get-tuple-element.167.refs_9_), channel_id=1, source_target_pairs={{0,8},{4,12},{24,16},{28,20},{8,0},{12,4},{16,24},{20,28},{1,9},{5... | collective-permute-start | bytes 786440 | tf_op jit(solution)/shard_map/ppermute | solution.py:256
  147.1 15.4 %collective-permute-start.41 = (f32[256,256]{1,0:T(8,128)S(1)}, f32[256,256]{1,0:T(8,128)S(1)}, u32[]{:S(2)}, u32[]{:S(2)}) collective-permute-start(f32[256,256]{1,0:T(8,128)S(1)} %get-tuple-element.173.refs_5_), channel_id=1, source_target_pairs={{0,8},{4,12},{24,16},{28,20},{8,0},{12,4},{16,24},{20,28},{1,9},{5... | collective-permute-start | bytes 786440 | tf_op jit(solution)/shard_map/ppermute | solution.py:256
  152.9 15.2 %collective-permute-start.42 = (f32[256,256]{1,0:T(8,128)S(1)}, f32[256,256]{1,0:T(8,128)S(1)}, u32[]{:S(2)}, u32[]{:S(2)}) collective-permute-start(f32[256,256]{1,0:T(8,128)S(1)} %get-tuple-element.176), channel_id=1, source_target_pairs={{8,0},{12,4},{16,24},{20,28},{9,1},{13,5},{17,25},{21,29},{10,2},{... | collective-permute-start | bytes 786440 | tf_op jit(solution)/shard_map/ppermute | solution.py:254
  156.9 16.5 %collective-permute-start.44 = (f32[256,256]{1,0:T(8,128)S(1)}, f32[256,256]{1,0:T(8,128)S(1)}, u32[]{:S(2)}, u32[]{:S(2)}) collective-permute-start(f32[256,256]{1,0:T(8,128)S(1)} %get-tuple-element.178.refs_5_), channel_id=1, source_target_pairs={{0,8},{4,12},{24,16},{28,20},{8,0},{12,4},{16,24},{20,28},{1,9},{5... | collective-permute-start | bytes 786440 | tf_op jit(solution)/shard_map/ppermute | solution.py:256
  (30 other events, 297.1 us)
